TPU v7x, 32 devices: a whole 2x2x4 slice. The times are simulated.
32 devices in a mesh: group: 8 (over y, x, core), tp: 4 (over z).
Axes of the slice: x: 2, y: 2, z: 4, core: 2. Of those that a mesh axis runs over, the one named last changes fastest.
Arguments:
- tokens: bfloat16 [6144, 8192], P('group', 'tp'), may hold values from -6 to 6
- w_query: bfloat16 [8192, 4096], P(None, 'tp'), may hold values from -0.0625 to 0.0625
- adapter_down: bfloat16 [96, 16, 8192], P('group', None, 'tp'), may hold values from -0.0625 to 0.0625
- adapter_up: bfloat16 [96, 16, 4096], P('group', None, 'tp'), may hold values from -1.5 to 1.5
- adapter_id: int32 [6144], P('group'), may hold values from 0 to 95, as said below
Outputs:
- query: bfloat16 [6144, 4096], P('group', 'tp')
Inputs may be any that keep to these rules, and one draw needn't show every extreme that they name: `adapter_id`: adapter a is owned by group a // 12. Among the 768 requests of one group (an aligned block), at most 192 use adapters of any one owner; in every draw one owner receives exactly 192 from every group.
All inputs are finite; a program needn't handle non-finite values.
Results may differ from a plain program's by a relative error of at most 0.014.
Values may be sent and summed in bfloat16 or wider, within the bound.
A program may use at most 192 MiB of HBM per device.

v0:
```python
import jax
import jax.numpy as jnp
from jax import lax
from jax.sharding import PartitionSpec as P

adapter_scale_factor = 2.0


def on_device(tokens, w_query, adapter_down, adapter_up, adapter_id):
    pool_down, pool_up = (
        lax.all_gather(adapter_down, "group", axis=0, tiled=True),
        lax.all_gather(adapter_up, "group", axis=0, tiled=True),
    )
    picked_down = jnp.take(pool_down, adapter_id, axis=0)
    partial_value = jnp.einsum(
        "nd,nrd->nr", tokens, picked_down, preferred_element_type=jnp.float32
    )
    total_output = lax.psum(partial_value, "tp")
    scaled_delta = (adapter_scale_factor * total_output).astype(jnp.bfloat16)
    picked_up = jnp.take(pool_up, adapter_id, axis=0)
    delta_rows = jnp.einsum(
        "nr,nrh->nh", scaled_delta, picked_up, preferred_element_type=jnp.float32
    ).astype(jnp.bfloat16)
    base = jnp.dot(
        lax.all_gather(tokens, "tp", axis=1, tiled=True),
        w_query,
        preferred_element_type=jnp.float32,
    )
    return (base + delta_rows.astype(jnp.float32)).astype(jnp.bfloat16)


def solution(mesh):
    placed = (
        P("group", "tp"),
        P(None, "tp"),
        P("group", None, "tp"),
        P("group", None, "tp"),
        P("group"),
    )
    return jax.shard_map(
        on_device, mesh=mesh, in_specs=placed, out_specs=P("group", "tp"), check_vma=False
    )
```

profile of v0, /device:TPU:10, one launch (start us, length us, event | category | flops | bytes accessed | tf_op | source)
XLA Modules:
  0.0 348.5 jit_solution(11789293602258993411)
XLA Ops:
  6.5 0.0 all-gather.8.cloned.1.call-start
  6.5 0.7 all-gather.8.cloned.1.call-update
  7.3 0.0 all-gather.6.cloned.1.call-start
  7.3 0.7 all-gather.6.cloned.1.call-update
  8.0 0.0 all-gather.4.cloned.1.call-start
  8.1 0.7 all-gather.4.cloned.1.call-update
  8.7 0.7 compare_select_fusion
  9.4 0.7 compare_and_fusion
  10.1 32.6 %all-gather.8.cloned.1.call-done = bf16[96,16,1024]{2,1,0:T(8,128)(2,1)} async-done(((bf16[12,16,1024]{2,1,0:T(8,128)(2,1)}), bf16[96,16,1024]{2,1,0:T(8,128)(2,1)}) %all-gather.8.cloned.1.call-update) | async-done | bytes 3145744 | tf_op jit(solution)/shard_map/all_gather | solution.py:12
  42.7 21.1 %gather_fusion.1 = bf16[768,16,1024]{2,1,0:T(8,128)(2,1)} fusion(bf16[96,16,1024]{2,1,0:T(8,128)(2,1)} %all-gather.8.cloned.1.call-done, s32[1024]{0:T(1024)S(1)} %pad_clamp_fusion), kind=kCustom, calls=%fused_computation.1 | custom fusion | bytes 50334720 | tf_op jit(solution)/shard_map/jit(_take)/gather | solution.py:20
  63.8 0.0 copy-start
  63.8 26.4 %all-gather.6.cloned.1.call-done = bf16[96,16,2048]{2,1,0:T(8,128)(2,1)} async-done(((bf16[12,16,2048]{2,1,0:T(8,128)(2,1)}), bf16[96,16,2048]{2,1,0:T(8,128)(2,1)}) %all-gather.6.cloned.1.call-update) | async-done | bytes 6291472 | tf_op jit(solution)/shard_map/all_gather | solution.py:11
  90.2 26.0 %gather_fusion = bf16[768,16,2048]{2,1,0:T(8,128)(2,1)} fusion(bf16[96,16,2048]{2,1,0:T(8,128)(2,1)} %all-gather.6.cloned.1.call-done, s32[1024]{0:T(1024)S(1)} %pad_clamp_fusion), kind=kCustom, calls=%fused_computation | custom fusion | bytes 100666368 | tf_op jit(solution)/shard_map/jit(_take)/gather | solution.py:14
  116.1 0.0 copy-done
  116.1 23.9 %fusion = f32[768,1,16]{2,1,0:T(1,128)S(1)} fusion(bf16[768,16,2048]{2,1,0:T(8,128)(2,1)} %gather_fusion, pred[768]{0:T(1024)(128)(4,1)S(1)} %compare_and_fusion, bf16[768,2048,1]{1,0,2:T(8,128)(2,1)S(1)} %bitcast.11), kind=kOutput, calls=%fused_computation.2 | convolution fusion | flops 75497472 | bytes 53527296 | tf_op jit(solution)/shard_map/nd,nrd->nr/dot_general | solution.py:15
  140.0 46.3 %psum.7 = f32[768,16]{1,0:T(8,128)S(1)} all-reduce(f32[768,16]{1,0:T(8,128)S(1)} %bitcast.12), channel_id=1, replica_groups=mesh['group'=8,'tp'=4] {'tp'}, use_global_device_ids=true, to_apply=%region_0.1 | all-reduce | flops 12288 | bytes 98304 | tf_op jit(solution)/shard_map/psum | solution.py:18
  186.3 13.4 %fusion.3 = bf16[768,1,1024]{2,1,0:T(2,128)(2,1)} fusion(bf16[768,16,1024]{2,1,0:T(8,128)(2,1)} %gather_fusion.1, pred[768]{0:T(1024)(128)(4,1)S(1)} %compare_and_fusion, bf16[768,16,1]{1,0,2:T(8,128)(2,1)S(1)} %fusion.10), kind=kOutput, calls=%fused_computation.5 | convolution fusion | flops 37748736 | bytes 26764032 | tf_op jit(solution)/shard_map/nr,nrh->nh/dot_general | solution.py:21
  199.7 120.1 %all-gather.4.cloned.1.call-done = bf16[768,8192]{1,0:T(8,128)(2,1)} async-done(((bf16[768,2048]{1,0:T(8,128)(2,1)}), bf16[768,8192]{1,0:T(8,128)(2,1)}) %all-gather.4.cloned.1.call-update) | async-done | bytes 12582928 | tf_op jit(solution)/shard_map/all_gather | solution.py:25
  319.8 22.1 %add_convert_fusion = bf16[768,1024]{1,0:T(8,128)(2,1)} fusion(bf16[768,8192]{1,0:T(8,128)(2,1)} %all-gather.4.cloned.1.call-done, bf16[8192,1024]{1,0:T(8,128)(2,1)} %param.6, bf16[768,1,1024]{2,1,0:T(2,128)(2,1)} %fusion.3), kind=kOutput, calls=%fused_computation.12 | convolution fusion | flops 12887261184 | bytes 32505856 | tf_op jit(solution)/shard_map/dot_general | solution.py:24
  (2 shorter events, 0.0 us)
Async XLA Ops:
  6.5 36.2 %all-gather.8.cloned.1.call-start = ((), (), s32[]{:S(2)}) async-start(), calls=%async_computation.2 | async-start | bytes 3538944 | tf_op jit(solution)/shard_map/all_gather | solution.py:12
  7.3 82.9 %all-gather.6.cloned.1.call-start = ((), (), s32[]{:S(2)}) async-start(), calls=%async_computation.1 | async-start | bytes 7077888 | tf_op jit(solution)/shard_map/all_gather | solution.py:11
  8.0 311.8 %all-gather.4.cloned.1.call-start = ((), (), s32[]{:S(2)}) async-start(), calls=%async_computation | async-start | bytes 15728640 | tf_op jit(solution)/shard_map/all_gather | solution.py:25
  63.8 52.3 %copy-start = (bf16[768,2048]{1,0:T(8,128)(2,1)S(1)}, bf16[768,2048]{1,0:T(8,128)(2,1)}, u32[]{:S(2)}) copy-start(bf16[768,2048]{1,0:T(8,128)(2,1)} %param.5) | copy-start | bytes 9437188
Sparse Core Ops, SparseCore 0:
  9.2 33.4 all-gather.7
  44.6 45.5 all-gather.5
  91.7 228.0 all-gather.3
where the time goes:
time: 353 us; the launch traced here: 348 us
  waiting for transfers between devices  181 us (51%)
  matrix products  59.4 us (17%)
  local copies, waits for them, and re-layouts  47 us (13%)
  blocking collectives  46.3 us (13%)
  between operations  13.1 us (4%)
    all_gather x1, waiting for transfers between devices, on_device(): lax.all_gather(tokens, 'tp', axis=1, tiled=True)  120 us
    psum x1, blocking collectives, on_device(): total_output = lax.psum(partial_value, 'tp')  46.3 us
    all_gather x1, waiting for transfers between devices, on_device(): lax.all_gather(adapter_up, 'group', axis=0, tiled=True)  32.6 us
    all_gather x1, waiting for transfers between devices, on_device(): lax.all_gather(adapter_down, 'group', axis=0, tiled=True)  26.4 us
    gather x1, local copies, waits for them, and re-layouts, on_device(): picked_down = jnp.take(pool_down, adapter_id, axis=0)  26 us
    dot_general x1, matrix products, on_device(): jnp.einsum('nd,nrd->nr', tokens, picked_down, preferred_element_type=jnp....  23.9 us
    dot_general x1, matrix products, on_device(): jnp.dot(lax.all_gather(tokens, 'tp', axis=1, tiled=True), w_query, prefer...  22.1 us
    gather x1, local copies, waits for them, and re-layouts, on_device(): picked_up = jnp.take(pool_up, adapter_id, axis=0)  21.1 us
  transfers between devices with their start and end apart: 3, of which 3 were waited for; matrix products, arithmetic and copies ran while one was open for 25% of the time, Pallas kernels for 0%

commit v1 on v0

v1 whole, which is shorter than its diff:
```python
import jax
import jax.numpy as jnp
from jax import lax
from jax.sharding import PartitionSpec as P

adapter_scale_factor = 2.0


def on_device(tokens, w_query, adapter_down, adapter_up, adapter_id):
    rows, depth = tokens.shape
    pool_down = lax.all_gather(adapter_down, "group", axis=0, tiled=True)
    pool_up = lax.all_gather(adapter_up, "group", axis=0, tiled=True)
    adapters, rank = pool_down.shape[:2]
    mine = jnp.arange(adapters, dtype=jnp.int32)[:, None] == adapter_id[None, :]
    every = lax.dot_general(
        pool_down.reshape(adapters * rank, depth),
        tokens,
        (((1,), (1,)), ((), ())),
        preferred_element_type=jnp.float32,
    ).reshape(adapters, rank, rows)
    partial_value = jnp.sum(jnp.where(mine[:, None, :], every, 0.0), axis=0)
    total_output = lax.psum(partial_value, "tp")
    scaled = (adapter_scale_factor * total_output).astype(jnp.bfloat16)
    spread = jnp.where(mine[:, None, :], scaled[None], jnp.zeros((), jnp.bfloat16))
    delta_rows = lax.dot_general(
        spread.reshape(adapters * rank, rows),
        pool_up.reshape(adapters * rank, -1),
        (((0,), (0,)), ((), ())),
        preferred_element_type=jnp.float32,
    ).astype(jnp.bfloat16)
    base = jnp.dot(
        lax.all_gather(tokens, "tp", axis=1, tiled=True),
        w_query,
        preferred_element_type=jnp.float32,
    )
    return (base + delta_rows.astype(jnp.float32)).astype(jnp.bfloat16)


def solution(mesh):
    placed = (
        P("group", "tp"),
        P(None, "tp"),
        P("group", None, "tp"),
        P("group", None, "tp"),
        P("group"),
    )
    return jax.shard_map(
        on_device, mesh=mesh, in_specs=placed, out_specs=P("group", "tp"), check_vma=False
    )
```

time: 353 us -> 338 us (0.958)
  waiting for transfers between devices: 181 us -> 262 us
  local copies, waits for them, and re-layouts: 47 us -> 0.01 us
  blocking collectives: 46.3 us -> 15.8 us
  matrix products: 59.4 us -> 42.6 us
    all_gather x1, waiting for transfers between devices: 120 us -> 210 us  [on_device(): lax.all_gather(tokens, 'tp', axis=1, tiled=True)]
    gather x2 -> x0, local copies, waits for them, and re-layouts: 47 us -> none  [the longest x1 26 us: on_device(): picked_down = jnp.take(pool_down, adapter_id, axis=0)]
    psum x1, blocking collectives: 46.3 us -> 15.8 us  [on_device(): total_output = lax.psum(partial_value, 'tp')]
    dot_general x2, matrix products: 37.3 us -> 22.5 us  [the longest x1 15.5 us: on_device(): lax.dot_general(pool_down.reshape(adapters * rank, depth), tokens, (((1,)...]
    all_gather x2, waiting for transfers between devices: 59 us -> 50 us  [the longest x1 47.1 us: on_device(): pool_down = lax.all_gather(adapter_down, 'group', axis=0, tiled=True)]
  transfers between devices with their start and end apart: 3 -> 3, of which waited for: 3 -> 3; matrix products, arithmetic and copies ran while one was open for 25% -> 7% of each run, Pallas kernels for 0% -> 0%
where the time goes in v1:
time: 338 us; the launch traced here: 334 us
  waiting for transfers between devices  262 us (78%)
  matrix products  42.6 us (13%)
  blocking collectives  15.8 us (5%)
  between operations  13.2 us (4%)
    all_gather x1, waiting for transfers between devices, on_device(): lax.all_gather(tokens, 'tp', axis=1, tiled=True)  210 us
    all_gather x1, waiting for transfers between devices, on_device(): pool_down = lax.all_gather(adapter_down, 'group', axis=0, tiled=True)  47.1 us
    dot_general x1, matrix products, on_device(): jnp.dot(lax.all_gather(tokens, 'tp', axis=1, tiled=True), w_query, prefer...  20 us
    psum x1, blocking collectives, on_device(): total_output = lax.psum(partial_value, 'tp')  15.8 us
    dot_general x1, matrix products, on_device(): lax.dot_general(pool_down.reshape(adapters * rank, depth), tokens, (((1,)...  15.5 us
    dot_general x1, matrix products, on_device(): lax.dot_general(spread.reshape(adapters * rank, rows), pool_up.reshape(ad...  7.02 us
  transfers between devices with their start and end apart: 3, of which 3 were waited for; matrix products, arithmetic and copies ran while one was open for 7% of the time, Pallas kernels for 0%

profile of v1, /device:TPU:10, one launch (start us, length us, event | category | flops | bytes accessed | tf_op | source)
XLA Modules:
  0.0 333.8 jit_solution(7460772517301558355)
XLA Ops:
  6.5 0.0 copy-start
  6.5 0.0 copy-start.1
  6.5 0.0 all-gather.6.cloned.1.call-start
  6.5 0.7 all-gather.6.cloned.1.call-update
  7.3 0.0 all-gather.8.cloned.1.call-start
  7.3 0.7 all-gather.8.cloned.1.call-update
  8.0 0.0 all-gather.4.cloned.1.call-start
  8.1 0.7 all-gather.4.cloned.1.call-update
  8.7 0.0 copy-done.1
  8.8 47.1 %all-gather.6.cloned.1.call-done = bf16[96,16,2048]{2,1,0:T(8,128)(2,1)} async-done(((bf16[12,16,2048]{2,1,0:T(8,128)(2,1)}), bf16[96,16,2048]{2,1,0:T(8,128)(2,1)}) %all-gather.6.cloned.1.call-update) | async-done | bytes 6291472 | tf_op jit(solution)/shard_map/all_gather | solution.py:11
  55.9 0.0 copy-done
  55.9 15.5 %select_reduce_fusion = f32[16,768]{1,0:T(8,128)S(1)} fusion(pred[96,768]{1,0:T(8,128)(4,1)S(1)} %iota_compare_fusion, bf16[768,2048]{1,0:T(8,128)(2,1)S(1)} %copy-done, bf16[96,16,2048]{2,1,0:T(8,128)(2,1)} %all-gather.6.cloned.1.call-done), kind=kOutput, calls=%fused_computation.2 | convolution fusion | flops 4834185216 | bytes 9560064 | tf_op jit(solution)/shard_map/dot_general | solution.py:15
  71.4 15.8 %psum.7 = f32[16,768]{1,0:T(8,128)S(1)} all-reduce(f32[16,768]{1,0:T(8,128)S(1)} %select_reduce_fusion), channel_id=1, replica_groups=mesh['group'=8,'tp'=4] {'tp'}, use_global_device_ids=true, to_apply=%region_1.2 | all-reduce | flops 12288 | bytes 98304 | tf_op jit(solution)/shard_map/psum | solution.py:22
  87.3 2.9 all-gather.8.cloned.1.call-done
  90.2 7.0 %bitcast_convert_fusion = bf16[768,1024]{1,0:T(8,128)(2,1)S(1)} fusion(bf16[96,16,1024]{2,1,0:T(8,128)(2,1)} %all-gather.8.cloned.1.call-done, pred[96,768]{1,0:T(8,128)(4,1)S(1)} %iota_compare_fusion, bf16[16,768]{1,0:T(8,128)(2,1)S(1)} %multiply_convert_fusion), kind=kOutput, calls=%fused_computation.3 | convolution fusion | flops 2417885184 | bytes 4816896 | tf_op jit(solution)/shard_map/dot_general | solution.py:25
  97.2 210.0 %all-gather.4.cloned.1.call-done = bf16[768,8192]{1,0:T(8,128)(2,1)} async-done(((bf16[768,2048]{1,0:T(8,128)(2,1)}), bf16[768,8192]{1,0:T(8,128)(2,1)}) %all-gather.4.cloned.1.call-update) | async-done | bytes 12582928 | tf_op jit(solution)/shard_map/all_gather | solution.py:32
  307.2 20.0 %add_convert_fusion = bf16[768,1024]{1,0:T(8,128)(2,1)} fusion(bf16[768,1024]{1,0:T(8,128)(2,1)S(1)} %bitcast_convert_fusion, bf16[768,8192]{1,0:T(8,128)(2,1)} %all-gather.4.cloned.1.call-done, bf16[8192,1024]{1,0:T(8,128)(2,1)} %param.6), kind=kOutput, calls=%fused_computation.7 | convolution fusion | flops 12887261184 | bytes 32505856 | tf_op jit(solution)/shard_map/dot_general | solution.py:31
  (2 shorter events, 0.1 us)
Async XLA Ops:
  6.5 49.4 %copy-start = (bf16[768,2048]{1,0:T(8,128)(2,1)S(1)}, bf16[768,2048]{1,0:T(8,128)(2,1)}, u32[]{:S(2)}) copy-start(bf16[768,2048]{1,0:T(8,128)(2,1)} %param.5) | copy-start | bytes 9437188
  6.5 2.2 copy-start.1
  6.5 49.4 %all-gather.6.cloned.1.call-start = ((), (), s32[]{:S(2)}) async-start(), calls=%async_computation.1 | async-start | bytes 7077888 | tf_op jit(solution)/shard_map/all_gather | solution.py:11
  7.3 82.9 %all-gather.8.cloned.1.call-start = ((), (), s32[]{:S(2)}) async-start(), calls=%async_computation.2 | async-start | bytes 3538944 | tf_op jit(solution)/shard_map/all_gather | solution.py:12
  8.0 299.2 %all-gather.4.cloned.1.call-start = ((), (), s32[]{:S(2)}) async-start(), calls=%async_computation | async-start | bytes 15728640 | tf_op jit(solution)/shard_map/all_gather | solution.py:32
Sparse Core Ops, SparseCore 0:
  9.2 46.6 all-gather.5
  57.8 32.3 all-gather.7
  91.7 215.4 all-gather.3

commit v2 on v1

--- a/solution.py
+++ b/solution.py
@@ -1,15 +1,232 @@
+import functools
+
 import jax
 import jax.numpy as jnp
 from jax import lax
+from jax.experimental import pallas as pl
+from jax.experimental.pallas import tpu as pltpu
 from jax.sharding import PartitionSpec as P
 
 adapter_scale_factor = 2.0
-
-
-def on_device(tokens, w_query, adapter_down, adapter_up, adapter_id):
+MESH = pl.DeviceIdType.MESH
+CHUNK = 256
+
+
+def bit_orders(m):
+    bits = m.bit_length() - 1
+    high = list(range(1, bits))
+    return [high + [0], high[::-1] + [0]]
+
+
+def place_of(g, order):
+    place = 0
+    for k, bit in enumerate(order):
+        place = place + lax.rem(lax.div(g, 1 << bit), 2) * (1 << k)
+    return place
+
+
+def flip(g, bit):
+    return g + (1 - 2 * lax.rem(lax.div(g, 1 << bit), 2)) * (1 << bit)
+
+
+def base_kernel(n, m, halves, tok, w_any, out, wbuf, rbuf, sbuf,
+                own_sem, zs, zr, ps, pr, rs, rr):
+    g, z = lax.axis_index("group"), lax.axis_index("tp")
+    depth = tok.shape[1]
+    rows = tok.shape[0]
+    chunks = rows // CHUNK
+    half_rows = depth // halves
+    piece = half_rows // m
+    orders = bit_orders(m)[:halves]
+    steps = m.bit_length() - 1
+    places = [place_of(g, order) for order in orders]
+
+    barrier = pltpu.get_barrier_semaphore()
+    for rel in range(1, n):
+        pl.semaphore_signal(barrier, inc=1, device_id=(g, lax.rem(z + rel, n)), device_id_type=MESH)
+    for bit in range(steps):
+        pl.semaphore_signal(barrier, inc=1, device_id=(flip(g, bit), z), device_id_type=MESH)
+    own = pltpu.make_async_copy(w_any.at[pl.ds(pl.multiple_of(z * depth, depth), depth)], wbuf.at[z], own_sem)
+    own.start()
+    pl.semaphore_wait(barrier, n - 1 + steps)
+
+    def inside(at):
+        return jnp.logical_and(at >= 0, at < n)
+
+    def span(h, k):
+        size = piece << k
+        at = h * half_rows + lax.div(places[h], 1 << k) * size
+        return pl.ds(pl.multiple_of(at, piece), size)
+
+    def z_copy(dist, s, h, target, block):
+        return pltpu.make_async_remote_copy(
+            src_ref=w_any.at[pl.ds(pl.multiple_of(target * depth + h * half_rows + places[h] * piece, piece), piece)],
+            dst_ref=wbuf.at[block, span(h, 0)],
+            send_sem=zs.at[dist - 1, s, h],
+            recv_sem=zr.at[dist - 1, s, h],
+            device_id=(g, target),
+            device_id_type=MESH,
+        )
+
+    def plane_copy(dist, s, h, k, block):
+        return pltpu.make_async_remote_copy(
+            src_ref=wbuf.at[block, span(h, k)],
+            dst_ref=wbuf.at[block, span(h, k)],
+            send_sem=ps.at[dist - 1, s, h, k],
+            recv_sem=pr.at[dist - 1, s, h, k],
+            device_id=(flip(g, orders[h][k]), z),
+            device_id_type=MESH,
+        )
+
+    def line_copy(dist, s, c):
+        sign = 1 - 2 * s
+        block = z + sign * dist
+        return pltpu.make_async_remote_copy(
+            src_ref=sbuf.at[block, c],
+            dst_ref=rbuf.at[s, dist - 1, c],
+            send_sem=rs.at[s, dist - 1, c],
+            recv_sem=rr.at[s, dist - 1, c],
+            device_id=(g, z + sign),
+            device_id_type=MESH,
+        )
+
+    def arrived(dist, s, c):
+        copy = pltpu.make_async_remote_copy(
+            src_ref=rbuf.at[s, dist, c],
+            dst_ref=rbuf.at[s, dist, c],
+            send_sem=rs.at[s, dist, c],
+            recv_sem=rr.at[s, dist, c],
+            device_id=(g, lax.rem(z + 1, n)),
+            device_id_type=MESH,
+        )
+        copy.wait_recv()
+
+    for dist in range(n - 1, 0, -1):
+        for s in range(2):
+            target = z + (1 - 2 * s) * dist
+
+            @pl.when(inside(target))
+            def _():
+                for h in range(halves):
+                    z_copy(dist, s, h, target, z).start()
+
+    own.wait()
+
+    @pl.loop(0, chunks)
+    def _(c):
+        at = pl.ds(pl.multiple_of(c * CHUNK, CHUNK), CHUNK)
+        out[at] = jnp.dot(tok[at], wbuf[z], preferred_element_type=jnp.float32)
+
+    def stage(dist, s, k):
+        block = z + (1 - 2 * s) * dist
+
+        @pl.when(inside(block))
+        def _():
+            for h in range(halves):
+                if k == 0:
+                    z_copy(dist, 1 - s, h, block, block).wait_recv()
+                else:
+                    plane_copy(dist, s, h, k - 1, block).wait_recv()
+                if k < steps:
+                    plane_copy(dist, s, h, k, block).start()
+
+    def reduce(dist, s):
+        sign = 1 - 2 * s
+        block = z + sign * dist
+
+        @pl.when(inside(block))
+        def _():
+            @pl.loop(0, chunks)
+            def _(c):
+                at = pl.ds(pl.multiple_of(c * CHUNK, CHUNK), CHUNK)
+                sbuf[block, c] = jnp.dot(
+                    tok[at], wbuf[block], preferred_element_type=jnp.float32
+                ).astype(jnp.bfloat16)
+
+                if dist < n - 1:
+                    @pl.when(inside(z - sign))
+                    def _():
+                        arrived(dist, s, c)
+                        sbuf[block, c] = (
+                            sbuf[block, c].astype(jnp.float32) + rbuf[s, dist, c].astype(jnp.float32)
+                        ).astype(jnp.bfloat16)
+
+                line_copy(dist, s, c).start()
+
+    for tick in range(n - 1 + steps):
+        for k in range(steps, -1, -1):
+            j = tick - k
+            if 0 <= j < n - 1:
+                for s in range(2):
+                    stage(n - 1 - j, s, k)
+        j = tick - steps
+        if 0 <= j < n - 1:
+            for s in range(2):
+                reduce(n - 1 - j, s)
+
+    for s in range(2):
+        @pl.when(inside(z - (1 - 2 * s)))
+        def _():
+            @pl.loop(0, chunks)
+            def _(c):
+                at = pl.ds(pl.multiple_of(c * CHUNK, CHUNK), CHUNK)
+                arrived(0, s, c)
+                out[at] = out[at] + rbuf[s, 0, c].astype(jnp.float32)
+
+    for dist in range(n - 1, 0, -1):
+        for s in range(2):
+            target = z + (1 - 2 * s) * dist
+
+            @pl.when(inside(target))
+            def _():
+                for h in range(halves):
+                    z_copy(dist, s, h, target, z).wait_send()
+                    for k in range(steps):
+                        plane_copy(dist, s, h, k, target).wait_send()
+
+                @pl.loop(0, chunks)
+                def _(c):
+                    line_copy(dist, s, c).wait_send()
+
+
+def base_call(n, m, tokens, w_query):
+    rows, depth = tokens.shape
+    columns = w_query.shape[1]
+    steps = m.bit_length() - 1
+    halves = 2 if depth % (2 * m * 16) == 0 else 1
+    chunks = rows // CHUNK
+    dma = pltpu.SemaphoreType.DMA
+    return pl.pallas_call(
+        functools.partial(base_kernel, n, m, halves),
+        out_shape=jax.ShapeDtypeStruct((rows, columns), jnp.float32),
+        in_specs=[pl.BlockSpec(memory_space=pltpu.VMEM), pl.BlockSpec(memory_space=pl.ANY)],
+        out_specs=pl.BlockSpec(memory_space=pltpu.VMEM),
+        scratch_shapes=[
+            pltpu.VMEM((n, depth, columns), jnp.bfloat16),
+            pltpu.VMEM((2, n - 1, chunks, CHUNK, columns), jnp.bfloat16),
+            pltpu.VMEM((n, chunks, CHUNK, columns), jnp.bfloat16),
+            dma,
+            dma((n - 1, 2, halves)),
+            dma((n - 1, 2, halves)),
+            dma((n - 1, 2, halves, steps)),
+            dma((n - 1, 2, halves, steps)),
+            dma((2, n - 1, chunks)),
+            dma((2, n - 1, chunks)),
+        ],
+        compiler_params=pltpu.CompilerParams(
+            collective_id=0, has_side_effects=True, vmem_limit_bytes=56 << 20
+        ),
+        cost_estimate=pl.CostEstimate(
+            flops=2 * rows * depth * n * columns, bytes_accessed=400 << 20, transcendentals=0
+        ),
+    )(tokens, w_query)
+
+
+def on_device(n, m, tokens, w_query, adapter_down, adapter_up, adapter_id):
     rows, depth = tokens.shape
     pool_down = lax.all_gather(adapter_down, "group", axis=0, tiled=True)
     pool_up = lax.all_gather(adapter_up, "group", axis=0, tiled=True)
+    base = base_call(n, m, tokens, w_query)
     adapters, rank = pool_down.shape[:2]
     mine = jnp.arange(adapters, dtype=jnp.int32)[:, None] == adapter_id[None, :]
     every = lax.dot_general(
@@ -28,11 +245,6 @@
         (((0,), (0,)), ((), ())),
         preferred_element_type=jnp.float32,
     ).astype(jnp.bfloat16)
-    base = jnp.dot(
-        lax.all_gather(tokens, "tp", axis=1, tiled=True),
-        w_query,
-        preferred_element_type=jnp.float32,
-    )
     return (base + delta_rows.astype(jnp.float32)).astype(jnp.bfloat16)
 
 
@@ -45,5 +257,9 @@
         P("group"),
     )
     return jax.shard_map(
-        on_device, mesh=mesh, in_specs=placed, out_specs=P("group", "tp"), check_vma=False
+        functools.partial(on_device, mesh.shape["tp"], mesh.shape["group"]),
+        mesh=mesh,
+        in_specs=placed,
+        out_specs=P("group", "tp"),
+        check_vma=False,
     )

time: 338 us -> 246 us (0.73)
  waiting for transfers between devices: 262 us -> 1.45 us
  Pallas kernels: 0 us -> 183 us
  matrix products: 42.6 us -> 26.6 us
    all_gather x1 -> x0, waiting for transfers between devices: 210 us -> none  [on_device(): lax.all_gather(tokens, 'tp', axis=1, tiled=True)]
    pallas_call x0 -> x1, Pallas kernels: none -> 183 us  [base_call(): pl.pallas_call(functools.partial(base_kernel, n, m, halves), out_shape=ja...]
    all_gather x1, waiting for transfers between devices: 47.1 us -> 0.02 us  [on_device(): pool_down = lax.all_gather(adapter_down, 'group', axis=0, tiled=True)]
    dot_general x1 -> x0, matrix products: 20 us -> none  [on_device(): jnp.dot(lax.all_gather(tokens, 'tp', axis=1, tiled=True), w_query, prefer...]
    dot_general x1, matrix products: 7.02 us -> 11.1 us  [on_device(): lax.dot_general(spread.reshape(adapters * rank, rows), pool_up.reshape(ad...]
  transfers between devices with their start and end apart: 3 -> 2, of which waited for: 3 -> 0; matrix products, arithmetic and copies ran while one was open for 7% -> 7% of each run, Pallas kernels for 0% -> 76%
where the time goes in v2:
time: 246 us; the launch traced here: 241 us
  Pallas kernels  183 us (74%)
  matrix products  26.6 us (11%)
  blocking collectives  16 us (7%)
  between operations  13.5 us (5%)
    pallas_call x1, Pallas kernels, base_call(): pl.pallas_call(functools.partial(base_kernel, n, m, halves), out_shape=ja...  183 us
    psum x1, blocking collectives, on_device(): total_output = lax.psum(partial_value, 'tp')  16 us
    dot_general x1, matrix products, on_device(): lax.dot_general(pool_down.reshape(adapters * rank, depth), tokens, (((1,)...  15.5 us
    dot_general x1, matrix products, on_device(): lax.dot_general(spread.reshape(adapters * rank, rows), pool_up.reshape(ad...  11.1 us
  transfers between devices with their start and end apart: 2, of which 0 were waited for; matrix products, arithmetic and copies ran while one was open for 7% of the time, Pallas kernels for 76%

profile of v2, /device:TPU:10, one launch (start us, length us, event | category | flops | bytes accessed | tf_op | source)
XLA Modules:
  0.0 241.1 jit_solution(5557707764636961948)
XLA Ops:
  6.5 0.0 all-gather.3.cloned.1.call-start
  6.5 0.7 all-gather.3.cloned.1.call-update
  7.3 0.0 all-gather.5.cloned.1.call-start
  7.3 0.7 all-gather.5.cloned.1.call-update
  8.0 0.7 iota_compare_fusion
  8.7 0.0 copy-start
  8.8 182.7 %shard_map.55 = f32[768,1024]{1,0:T(8,128)} custom-call(bf16[768,2048]{1,0:T(8,128)(2,1)} %tok.1, bf16[8192,1024]{1,0:T(8,128)(2,1)} %w_any.1), custom_call_target="tpu_custom_call" | custom-call | flops 12884901888 | bytes 419430400 | tf_op jit(solution)/shard_map/pallas_call | solution.py:199
  191.5 0.0 all-gather.3.cloned.1.call-done
  191.5 0.0 copy-done
  191.5 15.5 %select_reduce_fusion = f32[16,768]{1,0:T(8,128)S(1)} fusion(pred[96,768]{1,0:T(8,128)(4,1)S(1)} %iota_compare_fusion, bf16[768,2048]{1,0:T(8,128)(2,1)S(1)} %copy-done, bf16[96,16,2048]{2,1,0:T(8,128)(2,1)} %all-gather.3.cloned.1.call-done), kind=kOutput, calls=%fused_computation.2 | convolution fusion | flops 4834185216 | bytes 9560064 | tf_op jit(solution)/shard_map/dot_general | solution.py:232
  207.0 16.0 %psum.7 = f32[16,768]{1,0:T(8,128)S(1)} all-reduce(f32[16,768]{1,0:T(8,128)S(1)} %select_reduce_fusion), channel_id=1, replica_groups=mesh['group'=8,'tp'=4] {'tp'}, use_global_device_ids=true, to_apply=%region_1.2 | all-reduce | flops 12288 | bytes 98304 | tf_op jit(solution)/shard_map/psum | solution.py:239
  223.1 0.0 all-gather.5.cloned.1.call-done
  223.1 11.1 %add_convert_fusion = bf16[768,1024]{1,0:T(8,128)(2,1)} fusion(f32[768,1024]{1,0:T(8,128)} %shard_map.55, bf16[96,16,1024]{2,1,0:T(8,128)(2,1)} %all-gather.5.cloned.1.call-done, pred[96,768]{1,0:T(8,128)(4,1)S(1)} %iota_compare_fusion, bf16[16,768]{1,0:T(8,128)(2,1)S(1)} %multiply_convert_fusion), kind=kOutput, calls=%fused_computation.7 | convolution fusion | flops 2420244480 | bytes 7962624 | tf_op jit(solution)/shard_map/dot_general | solution.py:242
  (1 shorter events, 0.0 us)
Async XLA Ops:
  6.5 185.0 %all-gather.3.cloned.1.call-start = ((), (), s32[]{:S(2)}) async-start(), calls=%async_computation | async-start | bytes 7077888 | tf_op jit(solution)/shard_map/all_gather | solution.py:227
  7.3 215.8 %all-gather.5.cloned.1.call-start = ((), (), s32[]{:S(2)}) async-start(), calls=%async_computation.1 | async-start | bytes 3538944 | tf_op jit(solution)/shard_map/all_gather | solution.py:228
  8.7 182.8 %copy-start = (bf16[768,2048]{1,0:T(8,128)(2,1)S(1)}, bf16[768,2048]{1,0:T(8,128)(2,1)}, u32[]{:S(2)}) copy-start(bf16[768,2048]{1,0:T(8,128)(2,1)} %tok.1) | copy-start | bytes 9437188
Sparse Core Ops, SparseCore 0:
  9.2 69.4 all-gather.2
  80.6 40.9 all-gather.4

commit v3 on v2

--- a/solution.py
+++ b/solution.py
@@ -10,6 +10,7 @@
 adapter_scale_factor = 2.0
 MESH = pl.DeviceIdType.MESH
 CHUNK = 256
+UP_ROWS = 512
 
 
 def bit_orders(m):
@@ -29,8 +30,9 @@
     return g + (1 - 2 * lax.rem(lax.div(g, 1 << bit), 2)) * (1 << bit)
 
 
-def base_kernel(n, m, halves, tok, w_any, out, wbuf, rbuf, sbuf,
-                own_sem, zs, zr, ps, pr, rs, rr):
+def query_kernel(n, m, rank, halves, tok, w_any, down_any, up_any, id_row, id_column, out,
+                 total, wbuf, rbuf, sbuf, pool_down, pool_up, ranks,
+                 own_sem, pool_sem, zs, zr, ps, pr, rs, rr, qs, qr, ds, dr):
     g, z = lax.axis_index("group"), lax.axis_index("tp")
     depth = tok.shape[1]
     rows = tok.shape[0]
@@ -48,6 +50,21 @@
         pl.semaphore_signal(barrier, inc=1, device_id=(flip(g, bit), z), device_id_type=MESH)
     own = pltpu.make_async_copy(w_any.at[pl.ds(pl.multiple_of(z * depth, depth), depth)], wbuf.at[z], own_sem)
     own.start()
+    pools = (pool_down, pool_up)
+    owned = down_any.shape[0]
+    pool_orders = bit_orders(m)
+    pool_places = [place_of(g, order) for order in pool_orders]
+
+    def pool_span(i, k):
+        size = owned << k
+        return pl.ds(pl.multiple_of(lax.div(pool_places[i], 1 << k) * size, owned), size)
+
+    mine = [
+        pltpu.make_async_copy(source, pools[i].at[pool_span(i, 0)], pool_sem.at[i])
+        for i, source in enumerate((down_any, up_any))
+    ]
+    for copy in mine:
+        copy.start()
     pl.semaphore_wait(barrier, n - 1 + steps)
 
     def inside(at):
@@ -101,6 +118,83 @@
         )
         copy.wait_recv()
 
+    def pool_copy(i, k):
+        return pltpu.make_async_remote_copy(
+            src_ref=pools[i].at[pool_span(i, k)],
+            dst_ref=pools[i].at[pool_span(i, k)],
+            send_sem=qs.at[i, k],
+            recv_sem=qr.at[i, k],
+            device_id=(flip(g, pool_orders[i][k]), z),
+            device_id_type=MESH,
+        )
+
+    def rank_copy(rel):
+        return pltpu.make_async_remote_copy(
+            src_ref=ranks.at[0],
+            dst_ref=ranks.at[rel],
+            send_sem=ds.at[rel],
+            recv_sem=dr.at[rel],
+            device_id=(g, lax.rem(z + rel, n)),
+            device_id_type=MESH,
+        )
+
+    def pool_stage(k):
+        for i in range(2):
+            if k == 0:
+                mine[i].wait()
+            else:
+                pool_copy(i, k - 1).wait_recv()
+            if k < steps:
+                pool_copy(i, k).start()
+
+    def down_part():
+        ranks[0] = jnp.zeros((rank, rows), jnp.float32)
+
+        @pl.loop(0, pool_down.shape[0] // CHUNK)
+        def _(t):
+            at = pl.ds(pl.multiple_of(t * CHUNK, CHUNK), CHUNK)
+            every = lax.dot_general(
+                pool_down[at], tok[...], (((1,), (1,)), ((), ())), preferred_element_type=jnp.float32
+            )
+            kept = jnp.zeros((rank, rows), jnp.float32)
+            for a in range(CHUNK // rank):
+                kept = kept + jnp.where(
+                    id_row[...] == t * (CHUNK // rank) + a, every[a * rank:(a + 1) * rank], 0.0
+                )
+            ranks[0] += kept
+
+        for rel in range(1, n):
+            rank_copy(rel).start()
+
+    def up_part():
+        for rel in range(1, n):
+            rank_copy(rel).wait_recv()
+
+        copies = lax.broadcasted_iota(jnp.int32, (rank, UP_ROWS), 1) % rank
+        repeat = jnp.where(
+            copies == lax.broadcasted_iota(jnp.int32, (rank, UP_ROWS), 0), 1.0, 0.0
+        ).astype(jnp.bfloat16)
+        owner = lax.broadcasted_iota(jnp.int32, (CHUNK, UP_ROWS), 1) // rank
+
+        for c in range(chunks):
+            at = pl.ds(c * CHUNK, CHUNK)
+            down = ranks[0, :, at]
+            for rel in range(1, n):
+                down = down + ranks[rel, :, at]
+            scaled = jnp.transpose(adapter_scale_factor * down).astype(jnp.bfloat16)
+            spread = jnp.dot(scaled, repeat, preferred_element_type=jnp.float32)
+            ids = id_column[at]
+
+            def add(t, delta):
+                kept = jnp.where(ids == owner + t * (UP_ROWS // rank), spread, 0.0).astype(jnp.bfloat16)
+                these = pl.ds(pl.multiple_of(t * UP_ROWS, UP_ROWS), UP_ROWS)
+                return delta + jnp.dot(kept, pool_up[these], preferred_element_type=jnp.float32)
+
+            delta = lax.fori_loop(
+                0, pool_up.shape[0] // UP_ROWS, add, jnp.zeros((CHUNK, pool_up.shape[1]), jnp.float32)
+            )
+            total[at] += delta.astype(jnp.bfloat16).astype(jnp.float32)
+
     for dist in range(n - 1, 0, -1):
         for s in range(2):
             target = z + (1 - 2 * s) * dist
@@ -115,7 +209,7 @@
     @pl.loop(0, chunks)
     def _(c):
         at = pl.ds(pl.multiple_of(c * CHUNK, CHUNK), CHUNK)
-        out[at] = jnp.dot(tok[at], wbuf[z], preferred_element_type=jnp.float32)
+        total[at] = jnp.dot(tok[at], wbuf[z], preferred_element_type=jnp.float32)
 
     def stage(dist, s, k):
         block = z + (1 - 2 * s) * dist
@@ -153,16 +247,23 @@
 
                 line_copy(dist, s, c).start()
 
+    first_pool = n - 2
     for tick in range(n - 1 + steps):
         for k in range(steps, -1, -1):
             j = tick - k
             if 0 <= j < n - 1:
                 for s in range(2):
                     stage(n - 1 - j, s, k)
+        if tick >= first_pool:
+            pool_stage(tick - first_pool)
         j = tick - steps
+        if j == n - 2:
+            down_part()
         if 0 <= j < n - 1:
             for s in range(2):
                 reduce(n - 1 - j, s)
+
+    up_part()
 
     for s in range(2):
         @pl.when(inside(z - (1 - 2 * s)))
@@ -171,7 +272,7 @@
             def _(c):
                 at = pl.ds(pl.multiple_of(c * CHUNK, CHUNK), CHUNK)
                 arrived(0, s, c)
-                out[at] = out[at] + rbuf[s, 0, c].astype(jnp.float32)
+                total[at] += rbuf[s, 0, c].astype(jnp.float32)
 
     for dist in range(n - 1, 0, -1):
         for s in range(2):
@@ -188,64 +289,70 @@
                 def _(c):
                     line_copy(dist, s, c).wait_send()
 
-
-def base_call(n, m, tokens, w_query):
+    for i in range(2):
+        for k in range(steps):
+            pool_copy(i, k).wait_send()
+    for rel in range(1, n):
+        rank_copy(rel).wait_send()
+
+    @pl.loop(0, chunks)
+    def _(c):
+        at = pl.ds(pl.multiple_of(c * CHUNK, CHUNK), CHUNK)
+        out[at] = total[at].astype(out.dtype)
+
+
+def on_device(n, m, tokens, w_query, adapter_down, adapter_up, adapter_id):
     rows, depth = tokens.shape
     columns = w_query.shape[1]
+    owned, rank = adapter_down.shape[:2]
     steps = m.bit_length() - 1
     halves = 2 if depth % (2 * m * 16) == 0 else 1
     chunks = rows // CHUNK
+    down_id, up_id = (
+        place_of(adapter_id // owned, order) * owned + adapter_id % owned for order in bit_orders(m)
+    )
     dma = pltpu.SemaphoreType.DMA
+    vmem, anywhere = pl.BlockSpec(memory_space=pltpu.VMEM), pl.BlockSpec(memory_space=pl.ANY)
     return pl.pallas_call(
-        functools.partial(base_kernel, n, m, halves),
-        out_shape=jax.ShapeDtypeStruct((rows, columns), jnp.float32),
-        in_specs=[pl.BlockSpec(memory_space=pltpu.VMEM), pl.BlockSpec(memory_space=pl.ANY)],
-        out_specs=pl.BlockSpec(memory_space=pltpu.VMEM),
+        functools.partial(query_kernel, n, m, rank, halves),
+        out_shape=jax.ShapeDtypeStruct((rows, columns), jnp.bfloat16),
+        in_specs=[vmem, anywhere, anywhere, anywhere, vmem, vmem],
+        out_specs=vmem,
         scratch_shapes=[
+            pltpu.VMEM((rows, columns), jnp.float32),
             pltpu.VMEM((n, depth, columns), jnp.bfloat16),
             pltpu.VMEM((2, n - 1, chunks, CHUNK, columns), jnp.bfloat16),
             pltpu.VMEM((n, chunks, CHUNK, columns), jnp.bfloat16),
+            pltpu.VMEM((m * owned * rank, depth), jnp.bfloat16),
+            pltpu.VMEM((m * owned * rank, columns), jnp.bfloat16),
+            pltpu.VMEM((n, rank, rows), jnp.float32),
             dma,
+            dma((2,)),
             dma((n - 1, 2, halves)),
             dma((n - 1, 2, halves)),
             dma((n - 1, 2, halves, steps)),
             dma((n - 1, 2, halves, steps)),
             dma((2, n - 1, chunks)),
             dma((2, n - 1, chunks)),
+            dma((2, steps)),
+            dma((2, steps)),
+            dma((n,)),
+            dma((n,)),
         ],
         compiler_params=pltpu.CompilerParams(
-            collective_id=0, has_side_effects=True, vmem_limit_bytes=56 << 20
+            collective_id=0, has_side_effects=True, vmem_limit_bytes=60 << 20
         ),
         cost_estimate=pl.CostEstimate(
-            flops=2 * rows * depth * n * columns, bytes_accessed=400 << 20, transcendentals=0
+            flops=2 * rows * depth * n * columns, bytes_accessed=40 << 20, transcendentals=0
         ),
-    )(tokens, w_query)
-
-
-def on_device(n, m, tokens, w_query, adapter_down, adapter_up, adapter_id):
-    rows, depth = tokens.shape
-    pool_down = lax.all_gather(adapter_down, "group", axis=0, tiled=True)
-    pool_up = lax.all_gather(adapter_up, "group", axis=0, tiled=True)
-    base = base_call(n, m, tokens, w_query)
-    adapters, rank = pool_down.shape[:2]
-    mine = jnp.arange(adapters, dtype=jnp.int32)[:, None] == adapter_id[None, :]
-    every = lax.dot_general(
-        pool_down.reshape(adapters * rank, depth),
+    )(
         tokens,
-        (((1,), (1,)), ((), ())),
-        preferred_element_type=jnp.float32,
-    ).reshape(adapters, rank, rows)
-    partial_value = jnp.sum(jnp.where(mine[:, None, :], every, 0.0), axis=0)
-    total_output = lax.psum(partial_value, "tp")
-    scaled = (adapter_scale_factor * total_output).astype(jnp.bfloat16)
-    spread = jnp.where(mine[:, None, :], scaled[None], jnp.zeros((), jnp.bfloat16))
-    delta_rows = lax.dot_general(
-        spread.reshape(adapters * rank, rows),
-        pool_up.reshape(adapters * rank, -1),
-        (((0,), (0,)), ((), ())),
-        preferred_element_type=jnp.float32,
-    ).astype(jnp.bfloat16)
-    return (base + delta_rows.astype(jnp.float32)).astype(jnp.bfloat16)
+        w_query,
+        adapter_down.reshape(owned * rank, depth),
+        adapter_up.reshape(owned * rank, columns),
+        down_id[None, :],
+        up_id[:, None],
+    )
 
 
 def solution(mesh):

time: 246 us -> 210 us (0.85); the launches traced: 241 us -> 210 us
  matrix products: 26.6 us -> 0 us
  Pallas kernels: 183 us -> 205 us
  blocking collectives: 16 us -> 0 us
  between operations: 13.5 us -> 0.01 us
  local copies, waits for them, and re-layouts: 0.01 us -> 4.17 us
    dot_general x2 -> x0, matrix products: 26.6 us -> none  [the longest x1 15.5 us: on_device(): lax.dot_general(pool_down.reshape(adapters * rank, depth), tokens, (((1,)...]
    pallas_call x1, Pallas kernels: 183 us -> 205 us  [on_device(): pl.pallas_call(functools.partial(query_kernel, n, m, rank, halves), out_s...]
    psum x1 -> x0, blocking collectives: 16 us -> none  [on_device(): total_output = lax.psum(partial_value, 'tp')]
    unnamed x2 -> x1, local copies, waits for them, and re-layouts: 0.01 us -> 2.67 us
  transfers between devices with their start and end apart: 2 -> 0, of which waited for: 0 -> 0; matrix products, arithmetic and copies ran while one was open for 7% -> 0% of each run, Pallas kernels for 76% -> 0%
where the time goes in v3:
time: 210 us
  Pallas kernels  205 us (98%)
  local copies, waits for them, and re-layouts  4.17 us (2%)
    pallas_call x1, Pallas kernels, on_device(): pl.pallas_call(functools.partial(query_kernel, n, m, rank, halves), out_s...  205 us

profile of v3, /device:TPU:10, one launch (start us, length us, event | category | flops | bytes accessed | tf_op | source)
XLA Modules:
  0.0 209.8 jit_solution(1281589986115542201)
XLA Ops:
  0.0 0.7 multiply_add_fusion
  0.7 0.6 broadcast_in_dim.6.id_row
  1.3 0.9 broadcast_in_dim.8.id_column
  2.2 204.9 %shard_map.55 = bf16[768,1024]{1,0:T(8,128)(2,1)} custom-call(bf16[768,2048]{1,0:T(8,128)(2,1)} %tok.1, bf16[8192,1024]{1,0:T(8,128)(2,1)} %w_any.1, bf16[192,2048]{1,0:T(8,128)(2,1)} %bitcast.2, bf16[192,1024]{1,0:T(8,128)(2,1)} %bitcast.3, s32[1,768]{1,0:T(1,128)} %broadcast_in_dim.6.id_row, s32[768,1]{1,0:T(8,128)} %broadcast_in_dim.8.id_column), custom_call_target="tpu_custom_call" | custom-call | flops 12884901888 | bytes 41943040 | tf_op jit(solution)/shard_map/pallas_call | solution.py:316
  207.1 2.7 %copy.8 = bf16[768,1024]{1,0:T(8,128)(2,1)} copy(bf16[768,1024]{1,0:T(8,128)(2,1)} %shard_map.55) | data formatting | bytes 3145728

commit v4 on v3

--- a/solution.py
+++ b/solution.py
@@ -195,15 +195,20 @@
             )
             total[at] += delta.astype(jnp.bfloat16).astype(jnp.float32)
 
-    for dist in range(n - 1, 0, -1):
+    def weights_out(dist, begin):
         for s in range(2):
             target = z + (1 - 2 * s) * dist
 
             @pl.when(inside(target))
             def _():
                 for h in range(halves):
-                    z_copy(dist, s, h, target, z).start()
-
+                    copy = z_copy(dist, s, h, target, z)
+                    if begin:
+                        copy.start()
+                    else:
+                        copy.wait_send()
+
+    weights_out(n - 1, True)
     own.wait()
 
     @pl.loop(0, chunks)
@@ -249,6 +254,10 @@
 
     first_pool = n - 2
     for tick in range(n - 1 + steps):
+        if tick < n - 1:
+            weights_out(n - 1 - tick, False)
+        if tick < n - 2:
+            weights_out(n - 2 - tick, True)
         for k in range(steps, -1, -1):
             j = tick - k
             if 0 <= j < n - 1:
@@ -281,7 +290,6 @@
             @pl.when(inside(target))
             def _():
                 for h in range(halves):
-                    z_copy(dist, s, h, target, z).wait_send()
                     for k in range(steps):
                         plane_copy(dist, s, h, k, target).wait_send()
 

time: 210 us -> 223 us (1.062)
  Pallas kernels: 205 us -> 218 us
    pallas_call x1, Pallas kernels: 205 us -> 218 us  [on_device(): pl.pallas_call(functools.partial(query_kernel, n, m, rank, halves), out_s...]
where the time goes in v4:
time: 223 us
  Pallas kernels  218 us (98%)
  local copies, waits for them, and re-layouts  4.17 us (2%)
    pallas_call x1, Pallas kernels, on_device(): pl.pallas_call(functools.partial(query_kernel, n, m, rank, halves), out_s...  218 us

profile of v4, /device:TPU:10, one launch (start us, length us, event | category | flops | bytes accessed | tf_op | source)
XLA Modules:
  0.0 222.8 jit_solution(5096603121417985918)
XLA Ops:
  0.0 0.7 multiply_add_fusion
  0.7 0.6 broadcast_in_dim.6.id_row
  1.3 0.9 broadcast_in_dim.8.id_column
  2.2 217.9 %shard_map.55 = bf16[768,1024]{1,0:T(8,128)(2,1)} custom-call(bf16[768,2048]{1,0:T(8,128)(2,1)} %tok.1, bf16[8192,1024]{1,0:T(8,128)(2,1)} %w_any.1, bf16[192,2048]{1,0:T(8,128)(2,1)} %bitcast.2, bf16[192,1024]{1,0:T(8,128)(2,1)} %bitcast.3, s32[1,768]{1,0:T(1,128)} %broadcast_in_dim.6.id_row, s32[768,1]{1,0:T(8,128)} %broadcast_in_dim.8.id_column), custom_call_target="tpu_custom_call" | custom-call | flops 12884901888 | bytes 41943040 | tf_op jit(solution)/shard_map/pallas_call | solution.py:324
  220.1 2.7 %copy.8 = bf16[768,1024]{1,0:T(8,128)(2,1)} copy(bf16[768,1024]{1,0:T(8,128)(2,1)} %shard_map.55) | data formatting | bytes 3145728

commit v5 on v3

--- a/solution.py
+++ b/solution.py
@@ -31,7 +31,7 @@
 
 
 def query_kernel(n, m, rank, halves, tok, w_any, down_any, up_any, id_row, id_column, out,
-                 total, wbuf, rbuf, sbuf, pool_down, pool_up, ranks,
+                 total, wbuf, rbuf, sbuf, pool_down, pool_up, ranks, tok_t,
                  own_sem, pool_sem, zs, zr, ps, pr, rs, rr, qs, qr, ds, dr):
     g, z = lax.axis_index("group"), lax.axis_index("tp")
     depth = tok.shape[1]
@@ -153,9 +153,7 @@
         @pl.loop(0, pool_down.shape[0] // CHUNK)
         def _(t):
             at = pl.ds(pl.multiple_of(t * CHUNK, CHUNK), CHUNK)
-            every = lax.dot_general(
-                pool_down[at], tok[...], (((1,), (1,)), ((), ())), preferred_element_type=jnp.float32
-            )
+            every = jnp.dot(pool_down[at], tok_t[...], preferred_element_type=jnp.float32)
             kept = jnp.zeros((rank, rows), jnp.float32)
             for a in range(CHUNK // rank):
                 kept = kept + jnp.where(
@@ -210,6 +208,9 @@
     def _(c):
         at = pl.ds(pl.multiple_of(c * CHUNK, CHUNK), CHUNK)
         total[at] = jnp.dot(tok[at], wbuf[z], preferred_element_type=jnp.float32)
+
+    for c in range(chunks):
+        tok_t[:, c * CHUNK:(c + 1) * CHUNK] = jnp.transpose(tok[c * CHUNK:(c + 1) * CHUNK])
 
     def stage(dist, s, k):
         block = z + (1 - 2 * s) * dist
@@ -224,44 +225,45 @@
                 if k < steps:
                     plane_copy(dist, s, h, k, block).start()
 
-    def reduce(dist, s):
-        sign = 1 - 2 * s
-        block = z + sign * dist
-
-        @pl.when(inside(block))
-        def _():
-            @pl.loop(0, chunks)
-            def _(c):
-                at = pl.ds(pl.multiple_of(c * CHUNK, CHUNK), CHUNK)
-                sbuf[block, c] = jnp.dot(
-                    tok[at], wbuf[block], preferred_element_type=jnp.float32
-                ).astype(jnp.bfloat16)
-
-                if dist < n - 1:
-                    @pl.when(inside(z - sign))
-                    def _():
-                        arrived(dist, s, c)
-                        sbuf[block, c] = (
-                            sbuf[block, c].astype(jnp.float32) + rbuf[s, dist, c].astype(jnp.float32)
-                        ).astype(jnp.bfloat16)
-
-                line_copy(dist, s, c).start()
-
-    first_pool = n - 2
+    def reduce(dist):
+        @pl.loop(0, chunks)
+        def _(c):
+            at = pl.ds(pl.multiple_of(c * CHUNK, CHUNK), CHUNK)
+            for s in range(2):
+                sign = 1 - 2 * s
+                block = z + sign * dist
+
+                @pl.when(inside(block))
+                def _():
+                    sbuf[block, c] = jnp.dot(
+                        tok[at], wbuf[block], preferred_element_type=jnp.float32
+                    ).astype(jnp.bfloat16)
+
+                    if dist < n - 1:
+                        @pl.when(inside(z - sign))
+                        def _():
+                            arrived(dist, s, c)
+                            sbuf[block, c] = (
+                                sbuf[block, c].astype(jnp.float32) + rbuf[s, dist, c].astype(jnp.float32)
+                            ).astype(jnp.bfloat16)
+
+                    line_copy(dist, s, c).start()
+
+    down_tick = steps + min(1, n - 2)
+    first_pool = down_tick - steps
     for tick in range(n - 1 + steps):
         for k in range(steps, -1, -1):
             j = tick - k
             if 0 <= j < n - 1:
                 for s in range(2):
                     stage(n - 1 - j, s, k)
-        if tick >= first_pool:
+        if first_pool <= tick <= down_tick:
             pool_stage(tick - first_pool)
         j = tick - steps
-        if j == n - 2:
+        if tick == down_tick:
             down_part()
         if 0 <= j < n - 1:
-            for s in range(2):
-                reduce(n - 1 - j, s)
+            reduce(n - 1 - j)
 
     up_part()
 
@@ -326,6 +328,7 @@
             pltpu.VMEM((m * owned * rank, depth), jnp.bfloat16),
             pltpu.VMEM((m * owned * rank, columns), jnp.bfloat16),
             pltpu.VMEM((n, rank, rows), jnp.float32),
+            pltpu.VMEM((depth, rows), jnp.bfloat16),
             dma,
             dma((2,)),
             dma((n - 1, 2, halves)),

time: 210 us -> 221 us (1.052)
  Pallas kernels: 205 us -> 215 us
    pallas_call x1, Pallas kernels: 205 us -> 215 us  [on_device(): pl.pallas_call(functools.partial(query_kernel, n, m, rank, halves), out_s...]
where the time goes in v5:
time: 221 us; the launch traced here: 220 us
  Pallas kernels  215 us (97%)
  local copies, waits for them, and re-layouts  4.17 us (2%)
    pallas_call x1, Pallas kernels, on_device(): pl.pallas_call(functools.partial(query_kernel, n, m, rank, halves), out_s...  215 us

profile of v5, /device:TPU:10, one launch (start us, length us, event | category | flops | bytes accessed | tf_op | source)
XLA Modules:
  0.0 220.4 jit_solution(3794304665720368877)
XLA Ops:
  0.0 0.7 multiply_add_fusion
  0.7 0.6 broadcast_in_dim.6.id_row
  1.3 0.9 broadcast_in_dim.8.id_column
  2.2 215.5 %shard_map.55 = bf16[768,1024]{1,0:T(8,128)(2,1)} custom-call(bf16[768,2048]{1,0:T(8,128)(2,1)} %tok.1, bf16[8192,1024]{1,0:T(8,128)(2,1)} %w_any.1, bf16[192,2048]{1,0:T(8,128)(2,1)} %bitcast.2, bf16[192,1024]{1,0:T(8,128)(2,1)} %bitcast.3, s32[1,768]{1,0:T(1,128)} %broadcast_in_dim.6.id_row, s32[768,1]{1,0:T(8,128)} %broadcast_in_dim.8.id_column), custom_call_target="tpu_custom_call" | custom-call | flops 12884901888 | bytes 41943040 | tf_op jit(solution)/shard_map/pallas_call | solution.py:318
  217.7 2.7 %copy.8 = bf16[768,1024]{1,0:T(8,128)(2,1)} copy(bf16[768,1024]{1,0:T(8,128)(2,1)} %shard_map.55) | data formatting | bytes 3145728
